TPU v7x, 128 devices: a whole 4x4x4 slice. The times are simulated.
128 devices in a mesh: node: 32 (over y, x, z_lo), local: 4 (over z_hi, core).
Axes of the slice: x: 4, y: 4, z: 4 (z_hi: 2, z_lo: 2; z = z_hi * 2 + z_lo), core: 2. Of those that a mesh axis runs over, the one named last changes fastest.
Arguments:
- tokens: bfloat16 [16384, 4096], P(('node', 'local')), may hold values from -6 to 6
- grad_out: bfloat16 [16384, 4096], P(('node', 'local')), may hold values from -6 to 6
- router_logits: float32 [16384, 128], P(('node', 'local')), may hold values from -20 to 280
- group_id: int32 [16384], P(('node', 'local')), may hold values from 0 to 15, as said below
- expert_ids: int32 [16384, 2], P(('node', 'local')), may hold values from 0 to 7, as said below
- w_gate: bfloat16 [32, 4096, 1536], P('node', None, 'local'), may hold values from -0.09375 to 0.09375
- w_up: bfloat16 [32, 4096, 1536], P('node', None, 'local'), may hold values from -0.09375 to 0.09375
- w_down: bfloat16 [32, 1536, 4096], P('node', 'local'), may hold values from -0.15625 to 0.15625
Outputs:
- mixed: bfloat16 [16384, 4096], P(('node', 'local'))
- d_tokens: bfloat16 [16384, 4096], P(('node', 'local'))
- d_logits: float32 [16384, 128], P(('node', 'local'))
- grad_gate: bfloat16 [32, 4096, 1536], P('node', None, 'local')
- grad_up: bfloat16 [32, 4096, 1536], P('node', None, 'local')
- grad_down: bfloat16 [32, 1536, 4096], P('node', 'local')
Inputs may be any that keep to these rules, and one draw needn't show every extreme that they name: `group_id`: A token is computed here when its group is below 4. Among the tokens of one device no expert of those groups is named by more than 6 tokens, and one such expert is named by exactly 6 tokens of every device. `expert_ids`: the two numbers of a token differ; both name experts of the token's group.
All inputs are finite; a program needn't handle non-finite values.
Results may differ from a plain program's by a relative error of at most 0.0065.
Values may be sent and summed in bfloat16 or wider, within the bound.
No kernel may reach another device: no remote copies, remote signals or barrier semaphores. Data moves between devices by JAX's collectives and lax.ppermute only.
A program may use at most 192 MiB of HBM per device.

v0:
```python
import jax
import jax.numpy as jnp
from jax import lax
from jax.sharding import PartitionSpec as P

GSIZE = 8
CAP = 6


def cut_along(value, dim, length):
    lengths = value.shape
    pieces = value.reshape(*lengths[:dim], length, lengths[dim] // length, *lengths[dim + 1 :])
    return jnp.moveaxis(pieces, dim, 0)


def piece_ends(length, count):
    unit = 8 if length >= 8 * count else 1
    return [length // unit * k // count * unit for k in range(1, count)]


def in_order(pieces, dim):
    pieces = jnp.moveaxis(pieces, 0, dim)
    lengths = pieces.shape
    return pieces.reshape(*lengths[:dim], lengths[dim] * lengths[dim + 1], *lengths[dim + 2 :])


def exchange_in_pieces(value, axis, pieces, split_dim, concat_dim):
    blocks = cut_along(value, split_dim, lax.axis_size(axis))
    cut = max(range(1, max(2, blocks.ndim - 1)), key=lambda d: blocks.shape[d])
    outs = []
    for piece in jnp.split(blocks, piece_ends(blocks.shape[cut], pieces), axis=cut):
        if piece.size:
            outs.append(lax.all_to_all(piece, axis, split_axis=0, concat_axis=0, tiled=True))
    return in_order(jnp.concatenate(outs, axis=cut), concat_dim)


def gate_weights(logits, group_ids, chosen, inside):
    probabilities = jax.nn.softmax(logits, axis=-1)
    columns = jnp.arange(logits.shape[1], dtype=jnp.int32)
    member = ((columns // GSIZE)[None, :] == group_ids[:, None]).astype(logits.dtype)
    group_mass = jnp.sum(probabilities * member, axis=1)
    picked = jnp.sum(
        jnp.where(chosen[:, :, None] == columns[None, None, :], logits[:, None, :], 0.0), axis=2
    )
    pair_share = jax.nn.softmax(picked, axis=-1)
    return jnp.where(inside[:, None], group_mass[:, None] * pair_share, 0.0)


def spread(buffer):
    arrived = lax.all_to_all(buffer, "node", split_axis=0, concat_axis=2, tiled=True)
    arrived = lax.all_gather(arrived, "local", axis=2, tiled=True)
    return arrived[0]


def collect(partial_sums):
    summed = lax.psum_scatter(partial_sums[None], "local", scatter_dimension=2, tiled=True)
    result = exchange_in_pieces(summed.astype(jnp.bfloat16), "node", 2, 2, 0)
    return result.reshape(-1, result.shape[-1])


def body(tokens, grad_out, router_logits, group_id, expert_ids, w_gate, w_up, w_down):
    owned_count = w_gate.shape[0]
    node_count = lax.axis_size("node")
    expert_total = owned_count * node_count
    window_groups = expert_total // GSIZE
    model_width = tokens.shape[1]
    inside = group_id < window_groups
    chosen = group_id[:, None] * GSIZE + expert_ids
    target = jnp.where(inside[:, None], chosen, expert_total)
    expert_range = jnp.arange(expert_total, dtype=jnp.int32)
    onehot = (target[:, :, None] == expert_range[None, None, :]).astype(jnp.int32)
    per_token = jnp.sum(onehot, axis=1)
    earlier = jnp.cumsum(per_token, axis=0) - per_token
    slot_rank = jnp.sum(onehot * earlier[:, None, :], axis=2)
    slot_index = jnp.where(inside[:, None], target * CAP + slot_rank, -1)
    slot_range = jnp.arange(expert_total * CAP, dtype=jnp.int32)
    first_pick = (slot_range[:, None] == slot_index[None, :, 0]).astype(jnp.bfloat16)
    second_pick = (slot_range[:, None] == slot_index[None, :, 1]).astype(jnp.bfloat16)
    mix_weights, pull_back = jax.vjp(
        lambda values: gate_weights(values, group_id, chosen, inside), router_logits
    )
    grad_f32 = grad_out.astype(jnp.float32)
    first_grad = (mix_weights[:, 0:1] * grad_f32).astype(jnp.bfloat16)
    second_grad = (mix_weights[:, 1:2] * grad_f32).astype(jnp.bfloat16)
    send_rows = (
        jnp.dot(first_pick, tokens, preferred_element_type=jnp.float32)
        + jnp.dot(second_pick, tokens, preferred_element_type=jnp.float32)
    ).astype(jnp.bfloat16)
    send_grads = (
        jnp.dot(first_pick, first_grad, preferred_element_type=jnp.float32)
        + jnp.dot(second_pick, second_grad, preferred_element_type=jnp.float32)
    ).astype(jnp.bfloat16)
    buffer_shape = (node_count, owned_count, CAP, model_width)
    rows_in = spread(send_rows.reshape(buffer_shape))
    gate_pre = jnp.einsum("erd,edf->erf", rows_in, w_gate, preferred_element_type=jnp.float32)
    up_pre = jnp.einsum("erd,edf->erf", rows_in, w_up, preferred_element_type=jnp.float32)
    sigmoid_gate = jax.nn.sigmoid(gate_pre)
    activated = gate_pre * sigmoid_gate
    hidden = (activated * up_pre).astype(jnp.bfloat16)
    partial_out = jnp.einsum("erf,efd->erd", hidden, w_down, preferred_element_type=jnp.float32)
    out_flat = collect(partial_out)
    grads_in = spread(send_grads.reshape(buffer_shape))
    grad_hidden = jnp.einsum("erd,efd->erf", grads_in, w_down, preferred_element_type=jnp.float32)
    grad_gate_pre = (
        grad_hidden * up_pre * sigmoid_gate * (1.0 + gate_pre * (1.0 - sigmoid_gate))
    ).astype(jnp.bfloat16)
    grad_up_pre = (grad_hidden * activated).astype(jnp.bfloat16)
    partial_in = jnp.einsum(
        "erf,edf->erd", grad_gate_pre, w_gate, preferred_element_type=jnp.float32
    ) + jnp.einsum("erf,edf->erd", grad_up_pre, w_up, preferred_element_type=jnp.float32)
    back_flat = collect(partial_in)
    grad_gate = jnp.einsum(
        "erd,erf->edf", rows_in, grad_gate_pre, preferred_element_type=jnp.float32
    ).astype(jnp.bfloat16)
    grad_up = jnp.einsum(
        "erd,erf->edf", rows_in, grad_up_pre, preferred_element_type=jnp.float32
    ).astype(jnp.bfloat16)
    grad_down = jnp.einsum(
        "erf,erd->efd", hidden, grads_in, preferred_element_type=jnp.float32
    ).astype(jnp.bfloat16)
    first_out = jnp.einsum("st,sd->td", first_pick, out_flat, preferred_element_type=jnp.float32)
    second_out = jnp.einsum("st,sd->td", second_pick, out_flat, preferred_element_type=jnp.float32)
    first_back = jnp.einsum("st,sd->td", first_pick, back_flat, preferred_element_type=jnp.float32)
    second_back = jnp.einsum(
        "st,sd->td", second_pick, back_flat, preferred_element_type=jnp.float32
    )
    mixed = (mix_weights[:, 0:1] * first_out + mix_weights[:, 1:2] * second_out).astype(
        jnp.bfloat16
    )
    d_tokens = (first_back + second_back).astype(jnp.bfloat16)
    scores = jnp.stack(
        [jnp.sum(grad_f32 * first_out, axis=1), jnp.sum(grad_f32 * second_out, axis=1)], axis=1
    )
    d_logits = pull_back(scores)[0]
    return (mixed, d_tokens, d_logits, grad_gate, grad_up, grad_down)


def solution(mesh):
    return jax.shard_map(
        body,
        mesh=mesh,
        in_specs=(
            P(("node", "local"), None),
            P(("node", "local"), None),
            P(("node", "local"), None),
            P(("node", "local")),
            P(("node", "local"), None),
            P("node", None, "local"),
            P("node", None, "local"),
            P("node", "local", None),
        ),
        out_specs=(
            P(("node", "local"), None),
            P(("node", "local"), None),
            P(("node", "local"), None),
            P("node", None, "local"),
            P("node", None, "local"),
            P("node", "local", None),
        ),
        check_vma=False,
    )
```

profile of v0, /device:TPU:0, one launch (start us, length us, event | category | flops | bytes accessed | tf_op | source)
XLA Modules:
  0.0 582.0 jit_solution(17738413348024515923)
XLA Ops:
  17.0 37.9 %all_to_all.44 = bf16[32,1,6,4096]{3,2,1,0:T(8,128)(2,1)} all-to-all(bf16[32,1,6,4096]{3,2,1,0:T(8,128)(2,1)} %bitcast.95), channel_id=1, replica_groups=mesh['node'=32,'local'=4] {'node'}, dimensions={0} | all-to-all | bytes 3145728 | tf_op jit(solution)/shard_map/all_to_all | solution.py:50
  58.7 48.7 %all-gather.3.cloned.1.call-done = bf16[1,1,768,4096]{3,2,1,0:T(8,128)(2,1)} async-done(((bf16[1,1,192,4096]{3,2,1,0:T(8,128)(2,1)}), bf16[1,1,768,4096]{3,2,1,0:T(8,128)(2,1)}) %all-gather.3.cloned.1.call-update) | async-done | bytes 6291472 | tf_op jit(solution)/shard_map/all_gather | solution.py:51
  107.4 6.6 %fusion.10 = f32[768,384]{1,0:T(8,128)S(1)} fusion(bf16[1,1,768,4096]{3,2,1,0:T(8,128)(2,1)} %all-gather.3.cloned.1.call-done, bf16[1,4096,384]{2,1,0:T(8,128)(2,1)} %param.13), kind=kOutput, calls=%fused_computation.12 | convolution fusion | flops 2415919104 | bytes 10616832 | tf_op jit(solution)/shard_map/erd,edf->erf/dot_general | solution.py:95
  114.0 4.5 multiply_convert_fusion.2
  119.3 6.4 %convolution_bitcast_fusion = f32[1,1,768,4096]{3,2,1,0:T(8,128)} fusion(bf16[768,384]{1,0:T(8,128)(2,1)S(1)} %get-tuple-element.26, bf16[1,384,4096]{2,1,0:T(8,128)(2,1)S(1)} %copy-done), kind=kOutput, calls=%fused_computation.1 | convolution fusion | flops 2415919104 | bytes 16318464 | tf_op jit(solution)/shard_map/erf,efd->erd/dot_general | solution.py:100
  125.8 105.4 %reduce-scatter.3.cloned.1.call-done = f32[1,1,192,4096]{3,2,1,0:T(8,128)} async-done(((f32[1,1,768,4096]{3,2,1,0:T(8,128)}), f32[1,1,192,4096]{3,2,1,0:T(8,128)}) %reduce-scatter.3.cloned.1.call-update) | async-done | bytes 3145744 | tf_op jit(solution)/shard_map/reduce_scatter | solution.py:56
  237.9 4.7 slice_bitcast_fusion.3
  242.6 7.4 %all-to-all-start.1 = ((bf16[32,1,1,3,4096]{4,3,2,1,0:T(4,128)(2,1)}), bf16[32,1,1,3,4096]{4,3,2,1,0:T(4,128)(2,1)}, u32[]{:S(2)}, u32[]{:S(2)}) async-start(bf16[32,1,1,3,4096]{4,3,2,1,0:T(4,128)(2,1)} %get-tuple-element.18), calls=%async_computation.2 | async-start | bytes 2097152 | tf_op jit(solution)/shard_map/all_to_all | solution.py:33
  250.4 17.5 %all-to-all-done.1 = bf16[32,1,1,3,4096]{4,3,2,1,0:T(4,128)(2,1)} async-done(((bf16[32,1,1,3,4096]{4,3,2,1,0:T(4,128)(2,1)}), bf16[32,1,1,3,4096]{4,3,2,1,0:T(4,128)(2,1)}, u32[]{:S(2)}, u32[]{:S(2)}) %all-to-all-start.1) | async-done | bytes 786464 | tf_op jit(solution)/shard_map/all_to_all | solution.py:33
  267.9 4.7 all-to-all-start.2
  272.6 10.2 %all-gather.5.cloned.1.call-start = ((), (), s32[]{:S(2)}) async-start(), calls=%async_computation.10 | async-start | bytes 7864320 | tf_op jit(solution)/shard_map/all_gather | solution.py:51
  283.0 6.4 %all-to-all-done.2 = bf16[32,1,1,3,4096]{4,3,2,1,0:T(4,128)(2,1)} async-done(((bf16[32,1,1,3,4096]{4,3,2,1,0:T(4,128)(2,1)}), bf16[32,1,1,3,4096]{4,3,2,1,0:T(4,128)(2,1)}, u32[]{:S(2)}, u32[]{:S(2)}) %all-to-all-start.2) | async-done | bytes 786464 | tf_op jit(solution)/shard_map/all_to_all | solution.py:33
  289.4 3.9 pad_maximum_fusion
  307.6 31.9 %all_to_all.45 = bf16[32,1,6,4096]{3,2,1,0:T(8,128)(2,1)} all-to-all(bf16[32,1,6,4096]{3,2,1,0:T(8,128)(2,1)} %bitcast.96), channel_id=1, replica_groups=mesh['node'=32,'local'=4] {'node'}, dimensions={0} | all-to-all | bytes 3145728 | tf_op jit(solution)/shard_map/all_to_all | solution.py:50
  343.2 47.0 %all-gather.5.cloned.1.call-done = bf16[1,1,768,4096]{3,2,1,0:T(8,128)(2,1)} async-done(((bf16[1,1,192,4096]{3,2,1,0:T(8,128)(2,1)}), bf16[1,1,768,4096]{3,2,1,0:T(8,128)(2,1)}) %all-gather.5.cloned.1.call-update) | async-done | bytes 6291472 | tf_op jit(solution)/shard_map/all_gather | solution.py:51
  390.3 7.3 %multiply_convert_fusion = (bf16[768,384]{1,0:T(8,128)(2,1)S(1)}, bf16[768,384]{1,0:T(8,128)(2,1)S(1)}) fusion(f32[768,384]{1,0:T(8,128)} %copy-done.20, f32[768,384]{1,0:T(8,128)} %get-tuple-element.27, bf16[1,384,4096]{2,1,0:T(8,128)(2,1)S(1)} %copy-done, bf16[1,1,768,4096]{3,2,1,0:T(8,128)(2,1)} %all-gather.5.cloned.1.call-done), kind=kOutput, calls=%fused_computation.44 | convolution fusion | flops 2419752960 | bytes 12976128 | tf_op jit(solution)/shard_map/erd,efd->erf/dot_general | solution.py:103
  401.1 6.5 %add_bitcast_fusion = f32[1,1,768,4096]{3,2,1,0:T(8,128)} fusion(f32[768,4096]{1,0:T(8,128)S(1)} %fusion.37, bf16[768,384]{1,0:T(8,128)(2,1)S(1)} %get-tuple-element.14, bf16[1,4096,384]{2,1,0:T(8,128)(2,1)S(1)} %copy-done.11), kind=kOutput, calls=%fused_computation | convolution fusion | flops 2419064832 | bytes 28901376 | tf_op jit(solution)/shard_map/erf,edf->erd/dot_general | solution.py:110
  412.2 100.9 %reduce-scatter.5.cloned.1.call-done = f32[1,1,192,4096]{3,2,1,0:T(8,128)} async-done(((f32[1,1,768,4096]{3,2,1,0:T(8,128)}), f32[1,1,192,4096]{3,2,1,0:T(8,128)}) %reduce-scatter.5.cloned.1.call-update) | async-done | bytes 3145744 | tf_op jit(solution)/shard_map/reduce_scatter | solution.py:56
  521.2 7.5 %all-to-all-start.4 = ((bf16[32,1,1,3,4096]{4,3,2,1,0:T(4,128)(2,1)}), bf16[32,1,1,3,4096]{4,3,2,1,0:T(4,128)(2,1)S(1)}, u32[]{:S(2)}, u32[]{:S(2)}) async-start(bf16[32,1,1,3,4096]{4,3,2,1,0:T(4,128)(2,1)} %get-tuple-element.16), calls=%async_computation.6 | async-start | bytes 2097152 | tf_op jit(solution)/shard_map/all_to_all | solution.py:33
  529.5 7.9 %fusion.24 = bf16[1,4096,384]{2,1,0:T(8,128)(2,1)} fusion(bf16[768,384]{1,0:T(8,128)(2,1)S(1)} %copy-done.15, bf16[1,1,768,4096]{3,2,1,0:T(8,128)(2,1)} %all-gather.3.cloned.1.call-done), kind=kOutput, calls=%fused_computation.20 | convolution fusion | flops 2417491968 | bytes 10027008 | tf_op jit(solution)/shard_map/erd,erf->edf/dot_general | solution.py:115
  537.5 8.9 %all-to-all-done.4 = bf16[32,1,1,3,4096]{4,3,2,1,0:T(4,128)(2,1)S(1)} async-done(((bf16[32,1,1,3,4096]{4,3,2,1,0:T(4,128)(2,1)}), bf16[32,1,1,3,4096]{4,3,2,1,0:T(4,128)(2,1)S(1)}, u32[]{:S(2)}, u32[]{:S(2)}) %all-to-all-start.4) | async-done | bytes 786464 | tf_op jit(solution)/shard_map/all_to_all | solution.py:33
  546.4 4.7 all-to-all-start.5
  551.1 7.2 %fusion.21 = bf16[1,384,4096]{2,1,0:T(8,128)(2,1)} fusion(bf16[768,384]{1,0:T(8,128)(2,1)S(1)} %copy-done.9, bf16[1,1,768,4096]{3,2,1,0:T(8,128)(2,1)} %all-gather.5.cloned.1.call-done), kind=kOutput, calls=%fused_computation.19 | convolution fusion | flops 2417491968 | bytes 10027008 | tf_op jit(solution)/shard_map/erf,erd->efd/dot_general | solution.py:118
  558.3 7.9 %fusion.27 = bf16[1,4096,384]{2,1,0:T(8,128)(2,1)} fusion(bf16[768,384]{1,0:T(8,128)(2,1)S(1)} %copy-done.17, bf16[1,1,768,4096]{3,2,1,0:T(8,128)(2,1)} %all-gather.3.cloned.1.call-done), kind=kOutput, calls=%fused_computation.21 | convolution fusion | flops 2417491968 | bytes 10027008 | tf_op jit(solution)/shard_map/erd,erf->edf/dot_general | solution.py:112
  (100 shorter events, 65.5 us)
Async XLA Ops:
  7.2 112.2 %copy-start = (bf16[1,384,4096]{2,1,0:T(8,128)(2,1)S(1)}, bf16[1,384,4096]{2,1,0:T(8,128)(2,1)}, u32[]{:S(2)}) copy-start(bf16[1,384,4096]{2,1,0:T(8,128)(2,1)} %param.15) | copy-start | bytes 9437188
  7.2 100.2 %all-gather.3.cloned.1.call-start = ((), (), s32[]{:S(2)}) async-start(), calls=%async_computation.8 | async-start | bytes 7864320 | tf_op jit(solution)/shard_map/all_gather | solution.py:51
  58.6 172.6 %reduce-scatter.3.cloned.1.call-start = ((), (), s32[]{:S(2)}) async-start(), calls=%async_computation.9 | async-start | bytes 15728640 | tf_op jit(solution)/shard_map/reduce_scatter | solution.py:56
  107.4 6.6 %copy-start.10 = (bf16[1,4096,384]{2,1,0:T(8,128)(2,1)S(1)}, bf16[1,4096,384]{2,1,0:T(8,128)(2,1)}, u32[]{:S(2)}) copy-start(bf16[1,4096,384]{2,1,0:T(8,128)(2,1)} %param.14) | copy-start | bytes 9437188
  107.4 6.6 %copy-start.19 = (bf16[1,1,768,4096]{3,2,1,0:T(8,128)(2,1)S(1)}, bf16[1,1,768,4096]{3,2,1,0:T(8,128)(2,1)}, u32[]{:S(2)}) copy-start(bf16[1,1,768,4096]{3,2,1,0:T(8,128)(2,1)} %all-gather.3.cloned.1.call-done) | copy-start | bytes 18874372
  114.0 4.5 copy-start.20
  242.6 7.5 %copy-start.13 = (f32[128,128]{1,0:T(8,128)S(1)}, f32[128,128]{1,0:T(8,128)}, u32[]{:S(2)}) copy-start(f32[128,128]{1,0:T(8,128)} %param.10) | copy-start | bytes 196612
  242.6 25.3 %all-to-all-start.1 = ((bf16[32,1,1,3,4096]{4,3,2,1,0:T(4,128)(2,1)}), bf16[32,1,1,3,4096]{4,3,2,1,0:T(4,128)(2,1)}, u32[]{:S(2)}, u32[]{:S(2)}) async-start(bf16[32,1,1,3,4096]{4,3,2,1,0:T(4,128)(2,1)} %get-tuple-element.18), calls=%async_computation.2 | async-start | bytes 2097152 | tf_op jit(solution)/shard_map/all_to_all | solution.py:33
  267.9 21.5 %all-to-all-start.2 = ((bf16[32,1,1,3,4096]{4,3,2,1,0:T(4,128)(2,1)}), bf16[32,1,1,3,4096]{4,3,2,1,0:T(4,128)(2,1)}, u32[]{:S(2)}, u32[]{:S(2)}) async-start(bf16[32,1,1,3,4096]{4,3,2,1,0:T(4,128)(2,1)} %get-tuple-element.19), calls=%async_computation.3 | async-start | bytes 2097152 | tf_op jit(solution)/shard_map/all_to_all | solution.py:33
  272.6 117.7 %all-gather.5.cloned.1.call-start = ((), (), s32[]{:S(2)}) async-start(), calls=%async_computation.10 | async-start | bytes 7864320 | tf_op jit(solution)/shard_map/all_gather | solution.py:51
  297.0 2.2 copy-start.6
  299.1 2.2 copy-start.2
  299.1 2.2 copy-start.18
  343.2 169.9 %reduce-scatter.5.cloned.1.call-start = ((), (), s32[]{:S(2)}) async-start(), calls=%async_computation.11 | async-start | bytes 15728640 | tf_op jit(solution)/shard_map/reduce_scatter | solution.py:56
  390.3 7.3 %copy-start.12 = (bf16[1,4096,384]{2,1,0:T(8,128)(2,1)S(1)}, bf16[1,4096,384]{2,1,0:T(8,128)(2,1)}, u32[]{:S(2)}) copy-start(bf16[1,4096,384]{2,1,0:T(8,128)(2,1)} %param.13) | copy-start | bytes 9437188
  397.6 3.5 copy-start.16
  397.6 3.5 copy-start.14
  397.6 3.5 copy-start.11
  521.2 8.3 %copy-start.15 = (bf16[768,384]{1,0:T(8,128)(2,1)S(1)}, bf16[768,384]{1,0:T(8,128)(2,1)}, u32[]{:S(2)}) copy-start(bf16[768,384]{1,0:T(8,128)(2,1)} %copy-done.14) | copy-start | bytes 1769476
  521.2 25.2 %all-to-all-start.4 = ((bf16[32,1,1,3,4096]{4,3,2,1,0:T(4,128)(2,1)}), bf16[32,1,1,3,4096]{4,3,2,1,0:T(4,128)(2,1)S(1)}, u32[]{:S(2)}, u32[]{:S(2)}) async-start(bf16[32,1,1,3,4096]{4,3,2,1,0:T(4,128)(2,1)} %get-tuple-element.16), calls=%async_computation.6 | async-start | bytes 2097152 | tf_op jit(solution)/shard_map/all_to_all | solution.py:33
  537.5 13.6 %copy-start.9 = (bf16[768,384]{1,0:T(8,128)(2,1)S(1)}, bf16[768,384]{1,0:T(8,128)(2,1)}, u32[]{:S(2)}) copy-start(bf16[768,384]{1,0:T(8,128)(2,1)} %copy-done.8) | copy-start | bytes 1769476
  546.4 21.5 %all-to-all-start.5 = ((bf16[32,1,1,3,4096]{4,3,2,1,0:T(4,128)(2,1)}), bf16[32,1,1,3,4096]{4,3,2,1,0:T(4,128)(2,1)}, u32[]{:S(2)}, u32[]{:S(2)}) async-start(bf16[32,1,1,3,4096]{4,3,2,1,0:T(4,128)(2,1)} %get-tuple-element.17), calls=%async_computation.7 | async-start | bytes 2097152 | tf_op jit(solution)/shard_map/all_to_all | solution.py:33
  551.1 7.2 %copy-start.17 = (bf16[768,384]{1,0:T(8,128)(2,1)S(1)}, bf16[768,384]{1,0:T(8,128)(2,1)}, u32[]{:S(2)}) copy-start(bf16[768,384]{1,0:T(8,128)(2,1)} %copy-done.16) | copy-start | bytes 1769476
  571.6 3.5 copy-start.1
  (5 other events, 8.4 us)
Sparse Core Ops, SparseCore 0:
  58.7 48.6 all-gather.2
  125.9 105.2 reduce-scatter.2
  343.3 46.9 all-gather.4
  407.7 105.3 reduce-scatter.4
where the time goes:
time: 591 us; the launch traced here: 582 us
  waiting for transfers between devices  337 us (57%)
  matrix products  71.5 us (12%)
  blocking collectives  69.8 us (12%)
  local copies, waits for them, and re-layouts  35.1 us (6%)
  starting transfers between devices  34.6 us (6%)
  other arithmetic  19.9 us (3%)
  between operations  14.5 us (2%)
    reduce_scatter x2, waiting for transfers between devices, collect(): lax.psum_scatter(partial_sums[None], 'local', scatter_dimension=2, tiled=...  206 us
    all_gather x2, waiting for transfers between devices, spread(): arrived = lax.all_gather(arrived, 'local', axis=2, tiled=True)  95.8 us
    all_to_all x2, blocking collectives, spread(): lax.all_to_all(buffer, 'node', split_axis=0, concat_axis=2, tiled=True)  69.8 us
    all_to_all x4, waiting for transfers between devices, exchange_in_pieces(): lax.all_to_all(piece, axis, split_axis=0, concat_axis=0, tiled=True)  34.5 us
    all_to_all x4, starting transfers between devices, exchange_in_pieces(): lax.all_to_all(piece, axis, split_axis=0, concat_axis=0, tiled=True)  24.3 us
  transfers between devices with their start and end apart: 8, of which 8 were waited for; matrix products, arithmetic and copies ran while one was open for 5% of the time, Pallas kernels for 0%

commit v1 on v0

--- a/solution.py
+++ b/solution.py
@@ -5,6 +5,13 @@
 
 GSIZE = 8
 CAP = 6
+
+
+def stacked_exchange(x, name, split, join):
+    size = lax.axis_size(name)
+    parts = jnp.stack(jnp.split(x, size, axis=split), axis=0)
+    parts = lax.all_to_all(parts, name, split_axis=0, concat_axis=0)
+    return jnp.concatenate(parts, axis=join)
 
 
 def cut_along(value, dim, length):
@@ -47,7 +54,7 @@
 
 
 def spread(buffer):
-    arrived = lax.all_to_all(buffer, "node", split_axis=0, concat_axis=2, tiled=True)
+    arrived = stacked_exchange(buffer, "node", 0, 2)
     arrived = lax.all_gather(arrived, "local", axis=2, tiled=True)
     return arrived[0]
 

time: 591 us -> 582 us (0.985)
    all_to_all x2 -> x0, local copies, waits for them, and re-layouts: 7.32 us -> none  [spread(): lax.all_to_all(buffer, 'node', split_axis=0, concat_axis=2, tiled=True)]
where the time goes in v1:
time: 582 us; the launch traced here: 573 us
  waiting for transfers between devices  336 us (58%)
  matrix products  69.2 us (12%)
  blocking collectives  68.6 us (12%)
  starting transfers between devices  34.8 us (6%)
  local copies, waits for them, and re-layouts  29.3 us (5%)
  other arithmetic  19.9 us (3%)
  between operations  15 us (3%)
    reduce_scatter x2, waiting for transfers between devices, collect(): lax.psum_scatter(partial_sums[None], 'local', scatter_dimension=2, tiled=...  206 us
    all_gather x2, waiting for transfers between devices, spread(): arrived = lax.all_gather(arrived, 'local', axis=2, tiled=True)  95.8 us
    all_to_all x2, blocking collectives, stacked_exchange(): parts = lax.all_to_all(parts, name, split_axis=0, concat_axis=0)  68.6 us
    all_to_all x4, waiting for transfers between devices, exchange_in_pieces(): lax.all_to_all(piece, axis, split_axis=0, concat_axis=0, tiled=True)  34.3 us
    all_to_all x4, starting transfers between devices, exchange_in_pieces(): lax.all_to_all(piece, axis, split_axis=0, concat_axis=0, tiled=True)  24.3 us
  transfers between devices with their start and end apart: 8, of which 8 were waited for; matrix products, arithmetic and copies ran while one was open for 5% of the time, Pallas kernels for 0%

profile of v1, /device:TPU:0, one launch (start us, length us, event | category | flops | bytes accessed | tf_op | source)
XLA Modules:
  0.0 573.2 jit_solution(5687925408890282995)
XLA Ops:
  13.2 37.7 %all_to_all.30 = bf16[32,1,1,6,4096]{4,3,2,1,0:T(8,128)(2,1)} all-to-all(bf16[32,1,1,6,4096]{4,3,2,1,0:T(8,128)(2,1)S(1)} %constant_dynamic-update-slice_fusion), channel_id=1, replica_groups=mesh['node'=32,'local'=4] {'node'}, dimensions={0} | all-to-all | bytes 3145728 | tf_op jit(solution)/shard_map/all_to_all | solution.py:13
  54.7 48.7 %all-gather.3.cloned.1.call-done = bf16[1,1,768,4096]{3,2,1,0:T(8,128)(2,1)} async-done(((bf16[1,1,192,4096]{3,2,1,0:T(8,128)(2,1)}), bf16[1,1,768,4096]{3,2,1,0:T(8,128)(2,1)}) %all-gather.3.cloned.1.call-update) | async-done | bytes 6291472 | tf_op jit(solution)/shard_map/all_gather | solution.py:58
  103.4 6.6 %fusion.10 = f32[768,384]{1,0:T(8,128)S(1)} fusion(bf16[1,1,768,4096]{3,2,1,0:T(8,128)(2,1)} %all-gather.3.cloned.1.call-done, bf16[1,4096,384]{2,1,0:T(8,128)(2,1)} %param.13), kind=kOutput, calls=%fused_computation.12 | convolution fusion | flops 2415919104 | bytes 10616832 | tf_op jit(solution)/shard_map/erd,edf->erf/dot_general | solution.py:102
  110.0 4.5 multiply_convert_fusion.2
  115.3 6.4 %convolution_bitcast_fusion = f32[1,1,768,4096]{3,2,1,0:T(8,128)} fusion(bf16[768,384]{1,0:T(8,128)(2,1)S(1)} %get-tuple-element.26, bf16[1,384,4096]{2,1,0:T(8,128)(2,1)S(1)} %copy-done), kind=kOutput, calls=%fused_computation.1 | convolution fusion | flops 2415919104 | bytes 16318464 | tf_op jit(solution)/shard_map/erf,efd->erd/dot_general | solution.py:107
  121.8 105.4 %reduce-scatter.3.cloned.1.call-done = f32[1,1,192,4096]{3,2,1,0:T(8,128)} async-done(((f32[1,1,768,4096]{3,2,1,0:T(8,128)}), f32[1,1,192,4096]{3,2,1,0:T(8,128)}) %reduce-scatter.3.cloned.1.call-update) | async-done | bytes 3145744 | tf_op jit(solution)/shard_map/reduce_scatter | solution.py:63
  233.9 4.7 slice_bitcast_fusion.3
  238.6 7.5 %all-to-all-start.1 = ((bf16[32,1,1,3,4096]{4,3,2,1,0:T(4,128)(2,1)}), bf16[32,1,1,3,4096]{4,3,2,1,0:T(4,128)(2,1)}, u32[]{:S(2)}, u32[]{:S(2)}) async-start(bf16[32,1,1,3,4096]{4,3,2,1,0:T(4,128)(2,1)} %get-tuple-element.18), calls=%async_computation.2 | async-start | bytes 2097152 | tf_op jit(solution)/shard_map/all_to_all | solution.py:40
  246.4 17.5 %all-to-all-done.1 = bf16[32,1,1,3,4096]{4,3,2,1,0:T(4,128)(2,1)} async-done(((bf16[32,1,1,3,4096]{4,3,2,1,0:T(4,128)(2,1)}), bf16[32,1,1,3,4096]{4,3,2,1,0:T(4,128)(2,1)}, u32[]{:S(2)}, u32[]{:S(2)}) %all-to-all-start.1) | async-done | bytes 786464 | tf_op jit(solution)/shard_map/all_to_all | solution.py:40
  263.9 4.7 all-to-all-start.2
  268.6 10.4 %all-gather.5.cloned.1.call-start = ((), (), s32[]{:S(2)}) async-start(), calls=%async_computation.10 | async-start | bytes 7864320 | tf_op jit(solution)/shard_map/all_gather | solution.py:58
  279.2 6.2 %all-to-all-done.2 = bf16[32,1,1,3,4096]{4,3,2,1,0:T(4,128)(2,1)} async-done(((bf16[32,1,1,3,4096]{4,3,2,1,0:T(4,128)(2,1)}), bf16[32,1,1,3,4096]{4,3,2,1,0:T(4,128)(2,1)}, u32[]{:S(2)}, u32[]{:S(2)}) %all-to-all-start.2) | async-done | bytes 786464 | tf_op jit(solution)/shard_map/all_to_all | solution.py:40
  285.4 3.9 pad_maximum_fusion
  299.8 30.9 %all_to_all.31 = bf16[32,1,1,6,4096]{4,3,2,1,0:T(8,128)(2,1)} all-to-all(bf16[32,1,1,6,4096]{4,3,2,1,0:T(8,128)(2,1)S(1)} %constant_dynamic-update-slice_fusion.32), channel_id=1, replica_groups=mesh['node'=32,'local'=4] {'node'}, dimensions={0} | all-to-all | bytes 3145728 | tf_op jit(solution)/shard_map/all_to_all | solution.py:13
  334.4 47.0 %all-gather.5.cloned.1.call-done = bf16[1,1,768,4096]{3,2,1,0:T(8,128)(2,1)} async-done(((bf16[1,1,192,4096]{3,2,1,0:T(8,128)(2,1)}), bf16[1,1,768,4096]{3,2,1,0:T(8,128)(2,1)}) %all-gather.5.cloned.1.call-update) | async-done | bytes 6291472 | tf_op jit(solution)/shard_map/all_gather | solution.py:58
  381.4 7.3 %multiply_convert_fusion = (bf16[768,384]{1,0:T(8,128)(2,1)S(1)}, bf16[768,384]{1,0:T(8,128)(2,1)S(1)}) fusion(f32[768,384]{1,0:T(8,128)} %copy-done.20, f32[768,384]{1,0:T(8,128)} %get-tuple-element.27, bf16[1,384,4096]{2,1,0:T(8,128)(2,1)S(1)} %copy-done, bf16[1,1,768,4096]{3,2,1,0:T(8,128)(2,1)} %all-gather.5.cloned.1.call-done), kind=kOutput, calls=%fused_computation.44 | convolution fusion | flops 2419752960 | bytes 12976128 | tf_op jit(solution)/shard_map/erd,efd->erf/dot_general | solution.py:110
  392.2 6.5 %add_bitcast_fusion = f32[1,1,768,4096]{3,2,1,0:T(8,128)} fusion(f32[768,4096]{1,0:T(8,128)S(1)} %fusion.37, bf16[768,384]{1,0:T(8,128)(2,1)S(1)} %get-tuple-element.14, bf16[1,4096,384]{2,1,0:T(8,128)(2,1)S(1)} %copy-done.11), kind=kOutput, calls=%fused_computation | convolution fusion | flops 2419064832 | bytes 28901376 | tf_op jit(solution)/shard_map/erf,edf->erd/dot_general | solution.py:117
  403.3 100.9 %reduce-scatter.5.cloned.1.call-done = f32[1,1,192,4096]{3,2,1,0:T(8,128)} async-done(((f32[1,1,768,4096]{3,2,1,0:T(8,128)}), f32[1,1,192,4096]{3,2,1,0:T(8,128)}) %reduce-scatter.5.cloned.1.call-update) | async-done | bytes 3145744 | tf_op jit(solution)/shard_map/reduce_scatter | solution.py:63
  512.4 7.5 %all-to-all-start.4 = ((bf16[32,1,1,3,4096]{4,3,2,1,0:T(4,128)(2,1)}), bf16[32,1,1,3,4096]{4,3,2,1,0:T(4,128)(2,1)S(1)}, u32[]{:S(2)}, u32[]{:S(2)}) async-start(bf16[32,1,1,3,4096]{4,3,2,1,0:T(4,128)(2,1)} %get-tuple-element.16), calls=%async_computation.6 | async-start | bytes 2097152 | tf_op jit(solution)/shard_map/all_to_all | solution.py:40
  520.7 7.9 %fusion.24 = bf16[1,4096,384]{2,1,0:T(8,128)(2,1)} fusion(bf16[768,384]{1,0:T(8,128)(2,1)S(1)} %copy-done.15, bf16[1,1,768,4096]{3,2,1,0:T(8,128)(2,1)} %all-gather.3.cloned.1.call-done), kind=kOutput, calls=%fused_computation.20 | convolution fusion | flops 2417491968 | bytes 10027008 | tf_op jit(solution)/shard_map/erd,erf->edf/dot_general | solution.py:122
  528.6 8.9 %all-to-all-done.4 = bf16[32,1,1,3,4096]{4,3,2,1,0:T(4,128)(2,1)S(1)} async-done(((bf16[32,1,1,3,4096]{4,3,2,1,0:T(4,128)(2,1)}), bf16[32,1,1,3,4096]{4,3,2,1,0:T(4,128)(2,1)S(1)}, u32[]{:S(2)}, u32[]{:S(2)}) %all-to-all-start.4) | async-done | bytes 786464 | tf_op jit(solution)/shard_map/all_to_all | solution.py:40
  537.5 4.7 all-to-all-start.5
  542.2 7.2 %fusion.21 = bf16[1,384,4096]{2,1,0:T(8,128)(2,1)} fusion(bf16[768,384]{1,0:T(8,128)(2,1)S(1)} %copy-done.9, bf16[1,1,768,4096]{3,2,1,0:T(8,128)(2,1)} %all-gather.5.cloned.1.call-done), kind=kOutput, calls=%fused_computation.19 | convolution fusion | flops 2417491968 | bytes 10027008 | tf_op jit(solution)/shard_map/erf,erd->efd/dot_general | solution.py:125
  549.4 7.9 %fusion.27 = bf16[1,4096,384]{2,1,0:T(8,128)(2,1)} fusion(bf16[768,384]{1,0:T(8,128)(2,1)S(1)} %copy-done.17, bf16[1,1,768,4096]{3,2,1,0:T(8,128)(2,1)} %all-gather.3.cloned.1.call-done), kind=kOutput, calls=%fused_computation.21 | convolution fusion | flops 2417491968 | bytes 10027008 | tf_op jit(solution)/shard_map/erd,erf->edf/dot_general | solution.py:119
  (162 shorter events, 57.4 us)
Async XLA Ops:
  7.2 108.2 %copy-start = (bf16[1,384,4096]{2,1,0:T(8,128)(2,1)S(1)}, bf16[1,384,4096]{2,1,0:T(8,128)(2,1)}, u32[]{:S(2)}) copy-start(bf16[1,384,4096]{2,1,0:T(8,128)(2,1)} %param.15) | copy-start | bytes 9437188
  7.2 96.2 %all-gather.3.cloned.1.call-start = ((), (), s32[]{:S(2)}) async-start(), calls=%async_computation.8 | async-start | bytes 7864320 | tf_op jit(solution)/shard_map/all_gather | solution.py:58
  54.6 172.6 %reduce-scatter.3.cloned.1.call-start = ((), (), s32[]{:S(2)}) async-start(), calls=%async_computation.9 | async-start | bytes 15728640 | tf_op jit(solution)/shard_map/reduce_scatter | solution.py:63
  103.4 6.6 %copy-start.10 = (bf16[1,4096,384]{2,1,0:T(8,128)(2,1)S(1)}, bf16[1,4096,384]{2,1,0:T(8,128)(2,1)}, u32[]{:S(2)}) copy-start(bf16[1,4096,384]{2,1,0:T(8,128)(2,1)} %param.14) | copy-start | bytes 9437188
  103.4 6.6 %copy-start.19 = (bf16[1,1,768,4096]{3,2,1,0:T(8,128)(2,1)S(1)}, bf16[1,1,768,4096]{3,2,1,0:T(8,128)(2,1)}, u32[]{:S(2)}) copy-start(bf16[1,1,768,4096]{3,2,1,0:T(8,128)(2,1)} %all-gather.3.cloned.1.call-done) | copy-start | bytes 18874372
  110.0 4.5 copy-start.20
  238.6 7.5 %copy-start.13 = (f32[128,128]{1,0:T(8,128)S(1)}, f32[128,128]{1,0:T(8,128)}, u32[]{:S(2)}) copy-start(f32[128,128]{1,0:T(8,128)} %param.10) | copy-start | bytes 196612
  238.6 25.3 %all-to-all-start.1 = ((bf16[32,1,1,3,4096]{4,3,2,1,0:T(4,128)(2,1)}), bf16[32,1,1,3,4096]{4,3,2,1,0:T(4,128)(2,1)}, u32[]{:S(2)}, u32[]{:S(2)}) async-start(bf16[32,1,1,3,4096]{4,3,2,1,0:T(4,128)(2,1)} %get-tuple-element.18), calls=%async_computation.2 | async-start | bytes 2097152 | tf_op jit(solution)/shard_map/all_to_all | solution.py:40
  263.9 21.5 %all-to-all-start.2 = ((bf16[32,1,1,3,4096]{4,3,2,1,0:T(4,128)(2,1)}), bf16[32,1,1,3,4096]{4,3,2,1,0:T(4,128)(2,1)}, u32[]{:S(2)}, u32[]{:S(2)}) async-start(bf16[32,1,1,3,4096]{4,3,2,1,0:T(4,128)(2,1)} %get-tuple-element.19), calls=%async_computation.3 | async-start | bytes 2097152 | tf_op jit(solution)/shard_map/all_to_all | solution.py:40
  268.6 112.8 %all-gather.5.cloned.1.call-start = ((), (), s32[]{:S(2)}) async-start(), calls=%async_computation.10 | async-start | bytes 7864320 | tf_op jit(solution)/shard_map/all_gather | solution.py:58
  293.0 2.2 copy-start.6
  295.1 2.1 copy-start.2
  295.1 2.2 copy-start.18
  334.3 169.9 %reduce-scatter.5.cloned.1.call-start = ((), (), s32[]{:S(2)}) async-start(), calls=%async_computation.11 | async-start | bytes 15728640 | tf_op jit(solution)/shard_map/reduce_scatter | solution.py:63
  381.4 7.3 %copy-start.12 = (bf16[1,4096,384]{2,1,0:T(8,128)(2,1)S(1)}, bf16[1,4096,384]{2,1,0:T(8,128)(2,1)}, u32[]{:S(2)}) copy-start(bf16[1,4096,384]{2,1,0:T(8,128)(2,1)} %param.13) | copy-start | bytes 9437188
  388.7 3.5 copy-start.16
  388.7 3.5 copy-start.14
  388.7 3.5 copy-start.11
  512.4 8.3 %copy-start.15 = (bf16[768,384]{1,0:T(8,128)(2,1)S(1)}, bf16[768,384]{1,0:T(8,128)(2,1)}, u32[]{:S(2)}) copy-start(bf16[768,384]{1,0:T(8,128)(2,1)} %copy-done.14) | copy-start | bytes 1769476
  512.4 25.2 %all-to-all-start.4 = ((bf16[32,1,1,3,4096]{4,3,2,1,0:T(4,128)(2,1)}), bf16[32,1,1,3,4096]{4,3,2,1,0:T(4,128)(2,1)S(1)}, u32[]{:S(2)}, u32[]{:S(2)}) async-start(bf16[32,1,1,3,4096]{4,3,2,1,0:T(4,128)(2,1)} %get-tuple-element.16), calls=%async_computation.6 | async-start | bytes 2097152 | tf_op jit(solution)/shard_map/all_to_all | solution.py:40
  528.6 13.6 %copy-start.9 = (bf16[768,384]{1,0:T(8,128)(2,1)S(1)}, bf16[768,384]{1,0:T(8,128)(2,1)}, u32[]{:S(2)}) copy-start(bf16[768,384]{1,0:T(8,128)(2,1)} %copy-done.8) | copy-start | bytes 1769476
  537.5 21.5 %all-to-all-start.5 = ((bf16[32,1,1,3,4096]{4,3,2,1,0:T(4,128)(2,1)}), bf16[32,1,1,3,4096]{4,3,2,1,0:T(4,128)(2,1)}, u32[]{:S(2)}, u32[]{:S(2)}) async-start(bf16[32,1,1,3,4096]{4,3,2,1,0:T(4,128)(2,1)} %get-tuple-element.17), calls=%async_computation.7 | async-start | bytes 2097152 | tf_op jit(solution)/shard_map/all_to_all | solution.py:40
  542.2 7.2 %copy-start.17 = (bf16[768,384]{1,0:T(8,128)(2,1)S(1)}, bf16[768,384]{1,0:T(8,128)(2,1)}, u32[]{:S(2)}) copy-start(bf16[768,384]{1,0:T(8,128)(2,1)} %copy-done.16) | copy-start | bytes 1769476
  562.7 3.5 copy-start.1
  (5 other events, 8.4 us)
Sparse Core Ops, SparseCore 0:
  54.7 48.6 all-gather.2
  121.9 105.2 reduce-scatter.2
  334.4 46.9 all-gather.4
  398.9 105.3 reduce-scatter.4
